TPU v7x, 32 devices: a whole 2x2x4 slice. The times are simulated.
32 devices in a mesh: parts: 2 (over y), tile: 8 (over z, x), led: 2 (over core).
Axes of the slice: x: 2, y: 2, z: 4, core: 2. Of those that a mesh axis runs over, the one named last changes fastest.
Arguments:
- residual_spectra: bfloat16 [32, 2, 2048, 2048], P(('parts', 'led'), None, 'tile'), parts along dimension 0, may hold values from -6 to 6
- led_offsets: int32 [16, 2], P('led'), may hold values from -341 to 341
- pupil_radius: int32 [16], P('led'), may hold values from 409 to 512
- led_axial: float32 [16], P('led'), may hold values from 0.5 to 2
- depths: float32 [8], replicated, may hold values from -3 to 3
- slice_order: int32 [8], replicated, may hold values from 0 to 7, each once
- axial: float32 [2048, 2048], P('tile'), may hold values from 0 to 1.5
Outputs:
- gradient: float32 [16, 2, 2048, 2048], P('parts', None, ('tile', 'led')), parts along dimension 0
There are 2 independent parts, one for each index of `parts`. A program takes and returns all parts, laid end to end along the dimension named above; an argument that names none is the same for every part. Nothing has to cross between parts.
Inputs may be any that keep to these rules, and one draw needn't show every extreme that they name: `slice_order`: each output slice names a different depth slice.
All inputs are finite; a program needn't handle non-finite values.
Results may differ from a plain program's by a relative error of at most 0.0057.
Values may be sent and summed in bfloat16 or wider, within the bound.
A program may use at most 256 MiB of HBM per device.

v0:
```python
import math

import jax
import jax.numpy as jnp
from jax import lax
from jax.sharding import PartitionSpec as P


def signed_freq(index, length):
    return jnp.where(index < length // 2, index, index - length)


def dft_table(k_count, out_pos, length):
    k_index = jnp.arange(k_count, dtype=jnp.int32)
    phase_int = k_index[:, None] * out_pos[None, :] % length
    angles = phase_int.astype(jnp.float32) * (2.0 * math.pi / length)
    return jnp.stack([jnp.cos(angles), jnp.sin(angles)]).astype(jnp.bfloat16)


def masked_spectra(residual, offsets, radius, row_pos, length):
    freq_rows = signed_freq(row_pos, length)
    freq_cols = signed_freq(jnp.arange(length, dtype=jnp.int32), length)
    shift_rows = freq_rows[None, :] - offsets[:, 0:1]
    shift_cols = freq_cols[None, :] - offsets[:, 1:2]
    inside = shift_rows[:, :, None] ** 2 + shift_cols[:, None, :] ** 2 <= (radius**2)[:, None, None]
    return jnp.where(inside[:, None], residual, jnp.zeros_like(residual))


def select_depths(slice_order, depths):
    count = depths.shape[0]
    picker = (slice_order[:, None] == jnp.arange(count, dtype=jnp.int32)[None, :]).astype(
        jnp.float32
    )
    return jnp.dot(picker, depths, precision=lax.Precision.HIGHEST)


def mixing_weights(ordered, led_axial):
    phase_angle = ordered[:, None] * led_axial[None, :]
    cosine = jnp.cos(phase_angle)
    sine = jnp.sin(phase_angle)
    first = jnp.stack([cosine, sine], axis=-1)
    second = jnp.stack([-sine, cosine], axis=-1)
    return jnp.stack([first, second], axis=1).astype(jnp.bfloat16)


def apply_phase(summed, own_depths, axial):
    phase_angle = own_depths[:, None, None] * axial[None]
    cosine = jnp.cos(phase_angle)
    sine = jnp.sin(phase_angle)
    real_part = summed[:, 0] * cosine - summed[:, 1] * sine
    imag_part = summed[:, 0] * sine + summed[:, 1] * cosine
    return jnp.stack([real_part, imag_part], axis=1).astype(jnp.bfloat16)


def transform(spectra, out_pos, length, form):
    dft = dft_table(spectra.shape[-1], out_pos, length)
    products = jnp.einsum(form, spectra, dft, preferred_element_type=jnp.float32)
    real_part = products[:, 0, 0] - products[:, 1, 1]
    imag_part = products[:, 0, 1] + products[:, 1, 0]
    return jnp.stack([real_part, imag_part], axis=1)


def column_section(spectra, out_pos, length):
    out_count = out_pos.shape[0]
    block_size = min(256, out_count)
    pieces = [
        transform(spectra, out_pos[start : start + block_size], length, "jcak,tkm->jctma")
        for start in range(0, out_count, block_size)
    ]
    return jnp.concatenate(pieces, axis=2).astype(jnp.bfloat16)


def row_section(spectra, length):
    positions = jnp.arange(length, dtype=jnp.int32)
    block_size = min(256, length)
    pieces = [
        transform(spectra, positions[start : start + block_size], length, "jcak,tkm->jctam")
        for start in range(0, length, block_size)
    ]
    return jnp.concatenate(pieces, axis=3) * (1.0 / length)


def local(residual_spectra, led_offsets, pupil_radius, led_axial, depths, slice_order, axial):
    tile_rows = axial.shape[0]
    length = axial.shape[1]
    row_pos = lax.axis_index("tile") * tile_rows + jnp.arange(tile_rows, dtype=jnp.int32)
    masked = masked_spectra(residual_spectra, led_offsets, pupil_radius, row_pos, length)
    ordered = select_depths(slice_order, depths)
    weights = mixing_weights(ordered, led_axial)
    partial_value = jnp.einsum(
        "jolc,lcak->joak", weights, masked, preferred_element_type=jnp.float32
    )
    led_count = lax.axis_size("led")
    led_index = lax.axis_index("led")
    slice_count = depths.shape[0]
    summed = lax.psum_scatter(partial_value, "led", scatter_dimension=0, tiled=True)
    own_count = slice_count // led_count
    own_depths = lax.dynamic_slice_in_dim(ordered, led_index * own_count, own_count)
    phased = apply_phase(summed, own_depths, axial)
    half_done = column_section(phased, jnp.arange(length, dtype=jnp.int32), length)
    regrouped = lax.all_to_all(
        lax.all_to_all(half_done, "tile", split_axis=2, concat_axis=3, tiled=True),
        "led",
        split_axis=2,
        concat_axis=0,
        tiled=True,
    )
    gradient = row_section(regrouped, length)
    return gradient


def solution(mesh):
    placed = (
        P(("parts", "led"), None, "tile", None),
        P("led", None),
        P("led"),
        P("led"),
        P(),
        P(),
        P("tile", None),
    )
    return jax.shard_map(
        local,
        mesh=mesh,
        in_specs=placed,
        out_specs=P("parts", None, ("tile", "led"), None),
        check_vma=False,
    )
```

profile of v0, /device:TPU:10, one launch (start us, length us, event | category | flops | bytes accessed | tf_op | source)
XLA Modules:
  0.0 639.3 jit_solution(13278459115606042917)
XLA Ops:
  12.8 14.4 %broadcast_select_fusion = bf16[8,2,256,2048]{3,2,1,0:T(8,128)(2,1)} fusion(bf16[8,2,256,2048]{3,2,1,0:T(8,128)(2,1)} %param.7, pred[8,256,2048]{2,1,0:T(8,128)(4,1)S(1)} %add_compare_fusion), kind=kLoop, calls=%fused_computation.4 | loop fusion | flops 8388608 | bytes 37748736 | tf_op jit(solution)/shard_map/jit(_where)/select_n | solution.py:26
  27.3 34.1 %fusion.3 = f32[8,2,256,2048]{3,0,2,1:T(8,128)} fusion(bf16[8,2,256,2048]{3,2,1,0:T(8,128)(2,1)} %broadcast_select_fusion, bf16[8,1,8,2]{2,0,3,1:T(8,128)(2,1)S(1)} %get-tuple-element.36, bf16[8,1,8,2]{2,0,3,1:T(8,128)(2,1)S(1)} %get-tuple-element.35), kind=kOutput, calls=%fused_computation.5 | convolution fusion | flops 268436480 | bytes 50332160 | tf_op jit(solution)/shard_map/jolc,lcak->joak/dot_general | solution.py:90
  61.4 32.2 %copy.93 = f32[8,2,256,2048]{3,2,1,0:T(8,128)} copy(f32[8,2,256,2048]{3,0,2,1:T(8,128)} %fusion.3) | data formatting | bytes 67108864 | tf_op jit(solution)/shard_map/jolc,lcak->joak/dot_general | solution.py:90
  93.8 10.5 %cosine_convert_fusion.7 = (bf16[1,2048,256]{1,2,0:T(8,128)(2,1)}, bf16[1,2048,256]{1,2,0:T(8,128)(2,1)}) fusion(s32[256]{0:T(256)S(1)} %iota_add_fusion.7), kind=kLoop, calls=%fused_computation.155 | loop fusion | flops 8388608 | bytes 2098176 | tf_op jit(solution)/shard_map/convert.64
  104.3 9.6 %cosine_convert_fusion.6 = (bf16[1,2048,256]{1,2,0:T(8,128)(2,1)S(1)}, bf16[1,2048,256]{1,2,0:T(8,128)(2,1)}) fusion(s32[256]{0:T(256)S(1)} %iota_add_fusion.6), kind=kLoop, calls=%fused_computation.151 | loop fusion | flops 8388608 | bytes 2098176 | tf_op jit(solution)/shard_map/convert.52
  113.9 10.5 %cosine_convert_fusion.5 = (bf16[1,2048,256]{1,2,0:T(8,128)(2,1)}, bf16[1,2048,256]{1,2,0:T(8,128)(2,1)}) fusion(s32[256]{0:T(256)S(1)} %iota_add_fusion.5), kind=kLoop, calls=%fused_computation.147 | loop fusion | flops 8388608 | bytes 2098176 | tf_op jit(solution)/shard_map/convert.50
  124.4 10.5 %cosine_convert_fusion.4 = (bf16[1,2048,256]{1,2,0:T(8,128)(2,1)}, bf16[1,2048,256]{1,2,0:T(8,128)(2,1)}) fusion(s32[256]{0:T(256)S(1)} %iota_add_fusion.4), kind=kLoop, calls=%fused_computation.143 | loop fusion | flops 8388608 | bytes 2098176 | tf_op jit(solution)/shard_map/convert.48
  134.9 10.5 %cosine_convert_fusion.3 = (bf16[1,2048,256]{1,2,0:T(8,128)(2,1)}, bf16[1,2048,256]{1,2,0:T(8,128)(2,1)}) fusion(s32[256]{0:T(256)S(1)} %iota_add_fusion.3), kind=kLoop, calls=%fused_computation.139 | loop fusion | flops 8388608 | bytes 2098176 | tf_op jit(solution)/shard_map/convert.46
  145.4 10.5 %cosine_convert_fusion.2 = (bf16[1,2048,256]{1,2,0:T(8,128)(2,1)}, bf16[1,2048,256]{1,2,0:T(8,128)(2,1)}) fusion(s32[256]{0:T(256)S(1)} %iota_add_fusion.2), kind=kLoop, calls=%fused_computation.135 | loop fusion | flops 8388608 | bytes 2098176 | tf_op jit(solution)/shard_map/convert.44
  155.9 10.5 %cosine_convert_fusion.1 = (bf16[1,2048,256]{1,2,0:T(8,128)(2,1)}, bf16[1,2048,256]{1,2,0:T(8,128)(2,1)}) fusion(s32[256]{0:T(256)S(1)} %iota_add_fusion.1), kind=kLoop, calls=%fused_computation.131 | loop fusion | flops 8388608 | bytes 2098176 | tf_op jit(solution)/shard_map/convert.42
  166.4 10.5 %cosine_convert_fusion = (bf16[1,2048,256]{1,2,0:T(8,128)(2,1)}, bf16[1,2048,256]{1,2,0:T(8,128)(2,1)}) fusion(s32[256]{0:T(256)S(1)} %iota_add_fusion), kind=kLoop, calls=%fused_computation.127 | loop fusion | flops 8388608 | bytes 2098176 | tf_op jit(solution)/shard_map/convert.40
  176.9 34.1 %fusion.11 = (bf16[4,1,256,2048]{3,2,1,0:T(8,128)(2,1)S(1)}, bf16[4,1,256,2048]{3,2,1,0:T(8,128)(2,1)S(1)}) fusion(f32[4,2,256,2048]{3,2,1,0:T(8,128)} %reduce-scatter.2.cloned.1.call-done, f32[256,2048]{1,0:T(8,128)S(1)} %copy-done.10, f32[4]{0:T(128)S(1)} %dynamic_slice.3), kind=kLoop, calls=%fused_computation.13 | loop fusion | flops 18874368 | bytes 27262992 | tf_op jit(solution)/shard_map/convert.54
  216.9 4.6 fusion.42
  229.1 4.8 fusion.48
  247.5 4.9 fusion.57
  259.5 25.0 %copy.103 = bf16[4,2,2048,256]{3,0,1,2:T(4,128)(2,1)S(1)} copy(bf16[4,2,2048,256]{3,2,0,1:T(8,128)(2,1)S(1)} %maximum_dynamic-update-slice_fusion.8) | data formatting | bytes 16777216 | tf_op jit(solution)/shard_map/concatenate | solution.py:70
  284.5 187.0 %all_to_all.36 = bf16[4,2,2048,256]{3,0,1,2:T(4,128)(2,1)} all-to-all(bf16[4,2,2048,256]{3,0,1,2:T(4,128)(2,1)S(1)} %copy.103), channel_id=1, replica_groups=mesh['parts'=2,'tile'=8,'led'=2] {'tile'}, dimensions={2} | all-to-all | bytes 16777216 | tf_op jit(solution)/shard_map/all_to_all | solution.py:102
  471.5 8.5 %copy.104 = bf16[4,2,2048,256]{3,2,1,0:T(8,128)(2,1)} copy(bf16[4,2,2048,256]{3,0,1,2:T(4,128)(2,1)} %all_to_all.36) | data formatting | bytes 16777216 | tf_op jit(solution)/shard_map/all_to_all | solution.py:102
  480.0 11.4 %copy.105 = bf16[4,2,256,8,256]{2,4,3,1,0:T(8,128)(2,1)} copy(bf16[4,2,256,8,256]{4,2,3,1,0:T(8,128)(2,1)} %bitcast.222) | data formatting | bytes 16777216 | tf_op jit(solution)/shard_map/all_to_all | solution.py:102
  491.4 21.1 %copy.106 = bf16[4,2,256,2048]{3,1,0,2:T(2,128)(2,1)} copy(bf16[4,2,256,2048]{2,3,1,0:T(8,128)(2,1)} %bitcast.223) | data formatting | bytes 16777216 | tf_op jit(solution)/shard_map/all_to_all | solution.py:102
  512.5 18.6 %all_to_all.37 = bf16[4,2,256,2048]{3,1,0,2:T(2,128)(2,1)} all-to-all(bf16[4,2,256,2048]{3,1,0,2:T(2,128)(2,1)} %copy.106), channel_id=1, replica_groups=mesh['parts'=2,'tile'=8,'led'=2] {'led'}, dimensions={2} | all-to-all | bytes 16777216 | tf_op jit(solution)/shard_map/all_to_all | solution.py:101
  531.2 11.4 %copy.107 = bf16[4,2,256,2048]{3,2,1,0:T(8,128)(2,1)} copy(bf16[4,2,256,2048]{3,1,0,2:T(2,128)(2,1)} %all_to_all.37) | data formatting | bytes 16777216 | tf_op jit(solution)/shard_map/all_to_all | solution.py:101
  542.6 8.5 %copy.108 = bf16[2,4,2,128,2048]{4,3,2,1,0:T(8,128)(2,1)} copy(bf16[2,4,2,128,2048]{4,3,0,2,1:T(8,128)(2,1)} %bitcast.224) | data formatting | bytes 16777216 | tf_op jit(solution)/shard_map/all_to_all | solution.py:101
  551.1 7.9 %convolution_bitcast_fusion = f32[8,2,2,128,256]{3,4,1,0,2:T(8,128)S(1)} fusion(bf16[8,2,128,2048,1]{3,2,1,0,4:T(8,128)(2,1)} %bitcast.225, bf16[1,2048,256]{1,2,0:T(8,128)(2,1)S(1)} %copy-done.22, bf16[1,2048,256]{1,2,0:T(8,128)(2,1)S(1)} %copy-done.20), kind=kOutput, calls=%fused_computation.84 | convolution fusion | flops 4299161600 | bytes 14680064 | tf_op jit(solution)/shard_map/jcak,tkm->jctam/dot_general | solution.py:57
  560.5 6.1 fusion.63
  566.6 6.3 fusion.66
  573.0 4.5 fusion.69
  582.2 4.5 fusion.75
  586.7 4.8 fusion.78
  591.5 6.1 fusion.81
  609.5 6.1 broadcast_multiply_fusion
  615.6 16.4 %copy.118 = f32[8,2,128,2048]{3,2,1,0:T(8,128)} copy(f32[8,2,128,2048]{2,3,0,1:T(8,128)} %broadcast_multiply_fusion) | data formatting | bytes 33554432 | tf_op jit(solution)/shard_map/mul | solution.py:80
  (144 shorter events, 58.1 us)
Async XLA Ops:
  6.5 1.5 copy-start
  6.5 170.4 %reduce-scatter.2.cloned.1.call-start = ((), (), s32[]{:S(2)}) async-start(), calls=%async_computation.3 | async-start | bytes 50331648 | tf_op jit(solution)/shard_map/reduce_scatter | solution.py:96
  113.9 102.0 %copy-start.11 = (bf16[1,2048,256]{1,2,0:T(8,128)(2,1)}, bf16[1,2048,256]{1,2,0:T(8,128)(2,1)S(1)}, u32[]{:S(2)}) copy-start(bf16[1,2048,256]{1,2,0:T(8,128)(2,1)S(1)} %get-tuple-element.49) | copy-start | bytes 3145732
  134.9 42.0 %copy-start.10 = (f32[256,2048]{1,0:T(8,128)S(1)}, f32[256,2048]{1,0:T(8,128)}, u32[]{:S(2)}) copy-start(f32[256,2048]{1,0:T(8,128)} %param.13) | copy-start | bytes 6291460
  176.9 34.2 %copy-start.19 = (bf16[1,2048,256]{1,2,0:T(8,128)(2,1)S(1)}, bf16[1,2048,256]{1,2,0:T(8,128)(2,1)}, u32[]{:S(2)}) copy-start(bf16[1,2048,256]{1,2,0:T(8,128)(2,1)} %get-tuple-element.56) | copy-start | bytes 3145732
  176.9 34.2 %copy-start.21 = (bf16[1,2048,256]{1,2,0:T(8,128)(2,1)S(1)}, bf16[1,2048,256]{1,2,0:T(8,128)(2,1)}, u32[]{:S(2)}) copy-start(bf16[1,2048,256]{1,2,0:T(8,128)(2,1)} %get-tuple-element.57) | copy-start | bytes 3145732
  221.5 1.5 copy-start.17
  227.5 1.5 copy-start.25
  233.8 1.5 copy-start.29
  239.9 1.5 copy-start.33
  246.0 1.5 copy-start.37
  252.5 1.5 copy-start.40
  542.6 8.5 %copy-start.20 = (bf16[1,2048,256]{1,2,0:T(8,128)(2,1)S(1)}, bf16[1,2048,256]{1,2,0:T(8,128)(2,1)}, u32[]{:S(2)}) copy-start(bf16[1,2048,256]{1,2,0:T(8,128)(2,1)} %get-tuple-element.56) | copy-start | bytes 3145732
  542.6 8.5 %copy-start.22 = (bf16[1,2048,256]{1,2,0:T(8,128)(2,1)S(1)}, bf16[1,2048,256]{1,2,0:T(8,128)(2,1)}, u32[]{:S(2)}) copy-start(bf16[1,2048,256]{1,2,0:T(8,128)(2,1)} %get-tuple-element.57) | copy-start | bytes 3145732
  551.1 8.2 %copy-start.2 = (bf16[2,4,2,128,2048]{4,3,2,1,0:T(8,128)(2,1)S(1)}, bf16[2,4,2,128,2048]{4,3,2,1,0:T(8,128)(2,1)}, u32[]{:S(2)}) copy-start(bf16[2,4,2,128,2048]{4,3,2,1,0:T(8,128)(2,1)} %copy.108) | copy-start | bytes 25165828
  559.0 1.5 copy-start.14
  560.5 6.1 copy-start.16
  560.5 6.1 copy-start.18
  566.6 6.4 copy-start.24
  566.6 6.4 copy-start.26
  573.0 4.6 copy-start.28
  573.0 4.6 copy-start.30
  577.6 4.6 copy-start.32
  577.6 4.6 copy-start.34
  582.1 4.6 copy-start.36
  582.2 4.6 copy-start.38
  597.6 4.0 copy-start.3
  605.5 1.5 copy-start.9
  605.7 1.7 copy-start.6
  605.7 2.0 copy-start.7
  607.0 1.7 copy-start.5
  615.6 16.4 %copy-start.1 = (f32[8]{0:T(128)S(1)}, f32[8]{0:T(128)}, u32[]{:S(2)}) copy-start(f32[8]{0:T(128)} %param.11) | copy-start | bytes 100
  (10 other events, 12.4 us)
Sparse Core Ops, SparseCore 0:
  93.8 46.7 reduce-scatter.1
where the time goes:
time: 652 us; the launch traced here: 639 us
  blocking collectives  206 us (32%)
  other arithmetic  155 us (24%)
  local copies, waits for them, and re-layouts  148 us (23%)
  matrix products  117 us (18%)
  between operations  14.6 us (2%)
    all_to_all x1, blocking collectives, local(): lax.all_to_all(half_done, 'tile', split_axis=2, concat_axis=3, tiled=True)  187 us
    another operation x10, other arithmetic  118 us
    dot_general x16, matrix products, transform(): jnp.einsum(form, spectra, dft, preferred_element_type=jnp.float32)  81.7 us
    all_to_all x3, local copies, waits for them, and re-layouts, local(): lax.all_to_all(half_done, 'tile', split_axis=2, concat_axis=3, tiled=True)  41 us
    dot_general x1, matrix products, local(): jnp.einsum('jolc,lcak->joak', weights, masked, preferred_element_type=jnp...  34.1 us
    dot_general x1, local copies, waits for them, and re-layouts, local(): jnp.einsum('jolc,lcak->joak', weights, masked, preferred_element_type=jnp...  32.2 us
    concatenate x1, local copies, waits for them, and re-layouts, column_section(): return jnp.concatenate(pieces, axis=2).astype(jnp.bfloat16)  25 us
    all_to_all x2, local copies, waits for them, and re-layouts, local(): lax.all_to_all(lax.all_to_all(half_done, 'tile', split_axis=2, concat_axi...  19.9 us
  transfers between devices with their start and end apart: 1, of which 0 were waited for; matrix products, arithmetic and copies ran while one was open for 13% of the time, Pallas kernels for 0%

commit v1 on v0

--- a/solution.py
+++ b/solution.py
@@ -1,9 +1,18 @@
+import functools
 import math
 
 import jax
 import jax.numpy as jnp
+import ml_dtypes
+import numpy as np
 from jax import lax
+from jax.experimental import pallas as pl
+from jax.experimental.pallas import tpu as pltpu
 from jax.sharding import PartitionSpec as P
+
+LANES = 128
+GROUP = 16
+MESH = pl.DeviceIdType.MESH
 
 
 def signed_freq(index, length):
@@ -109,6 +118,304 @@
     return gradient
 
 
+def full_table(length):
+    phase_int = np.outer(np.arange(length), np.arange(length)) % length
+    angles = np.arange(length).astype(np.float64) * (2.0 * math.pi / length)
+    pair = np.stack([np.cos(angles), np.sin(angles)]).astype(np.float32).astype(ml_dtypes.bfloat16)
+    return pair[:, phase_int]
+
+
+def useful_edge(length):
+    reach = length // 6 + length // 4
+    return -(-(reach + 1) // LANES) * LANES
+
+
+def sine_cosine(angle):
+    quarter = angle * 0.25
+    z = quarter * quarter
+    sine = quarter * (1.0 + z * (-1 / 6 + z * (1 / 120 + z * (-1 / 5040 + z * (1 / 362880)))))
+    cosine = 1.0 + z * (
+        -1 / 2 + z * (1 / 24 + z * (-1 / 720 + z * (1 / 40320 - z * (1 / 3628800))))
+    )
+    for _ in range(2):
+        sine, cosine = 2.0 * sine * cosine, 1.0 - 2.0 * sine * sine
+    return sine, cosine
+
+
+def mix_kernel(length, edge, ints, depths, weights, own, peer, axial, out):
+    own_leds, peer_leds = own.shape[0], peer.shape[0]
+    leds = own_leds + peer_leds
+    slices = out.shape[0]
+    row = ints[1] + pl.program_id(0) * GROUP + lax.broadcasted_iota(jnp.int32, (GROUP, 1), 0)
+    freq_row = jnp.where(row < length // 2, row, row - length)
+    lane = lax.broadcasted_iota(jnp.int32, (1, edge), 1)
+    for half in range(2):
+        start = 0 if half == 0 else length - edge
+        freq_col = lane if half == 0 else lane - edge
+        planes = []
+        for led in range(leds):
+            shift_row = freq_row - ints[2 + led]
+            shift_col = freq_col - ints[2 + leds + led]
+            room = ints[2 + 2 * leds + led] - shift_row * shift_row
+            inside = jnp.where(shift_col * shift_col <= room, 1.0, 0.0).astype(jnp.bfloat16)
+            for part in range(2):
+                if led < own_leds:
+                    values = own[led, part, :, start : start + edge]
+                else:
+                    values = peer[led - own_leds, part, :, half * edge : (half + 1) * edge]
+                planes.append(values * inside)
+        stacked = jnp.concatenate(planes, axis=0)
+        summed = jnp.dot(weights[...], stacked, preferred_element_type=jnp.float32)
+        wave = axial[:, start : start + edge]
+        for j in range(slices):
+            real = summed[(2 * j) * GROUP : (2 * j + 1) * GROUP]
+            imag = summed[(2 * j + 1) * GROUP : (2 * j + 2) * GROUP]
+            sine, cosine = sine_cosine(depths[j] * wave)
+            where = slice(half * edge, (half + 1) * edge)
+            out[j, 0, :, where] = (real * cosine - imag * sine).astype(jnp.bfloat16)
+            out[j, 1, :, where] = (real * sine + imag * cosine).astype(jnp.bfloat16)
+
+
+def transform_kernel(
+    length,
+    edge,
+    table_hbm,
+    phased_hbm,
+    out_hbm,
+    table,
+    phased,
+    send,
+    recv,
+    result,
+    load_sem,
+    phased_sem,
+    send_sem,
+    recv_sem,
+    out_sem,
+):
+    slices = phased.shape[0]
+    count = length // LANES
+    dead_first, dead_last = edge // LANES, count - edge // LANES
+    led_count = lax.axis_size("led")
+    part = lax.axis_index("parts")
+    me = lax.axis_index("tile") * led_count + lax.axis_index("led")
+
+    def place(device):
+        return (part, device // led_count, device % led_count)
+
+    table_load = pltpu.make_async_copy(table_hbm, table, load_sem)
+    table_load.start()
+    phased_load = pltpu.make_async_copy(phased_hbm, phased, phased_sem)
+    phased_load.start()
+
+    barrier = pltpu.get_barrier_semaphore()
+
+    @pl.loop(1, count)
+    def _(step):
+        pl.semaphore_signal(
+            barrier, inc=1, device_id=place((me + step) % count), device_id_type=MESH
+        )
+
+    pl.semaphore_wait(barrier, count - 1)
+    phased_load.wait()
+    table_load.wait()
+
+    def lanes_of(device):
+        return pl.ds(pl.multiple_of(device * LANES, LANES), LANES)
+
+    def remote(j, device):
+        return pltpu.make_async_remote_copy(
+            src_ref=send.at[j, device],
+            dst_ref=recv.at[j, :, lanes_of(me)],
+            send_sem=send_sem.at[j, device],
+            recv_sem=recv_sem.at[j, me],
+            device_id=place(device),
+            device_id_type=MESH,
+        )
+
+    def landing(j, device):
+        return pltpu.make_async_copy(
+            send.at[j, device], recv.at[j, :, lanes_of(device)], recv_sem.at[j, device]
+        )
+
+    has_rows = jnp.logical_or(me < dead_first, me >= dead_last)
+    quad = 4
+    groups = count // quad
+
+    @pl.when(has_rows)
+    def _():
+        @pl.loop(0, slices)
+        def _(j):
+            spectra = phased[j]
+
+            @pl.loop(0, groups)
+            def _(step):
+                group = (me // quad + groups // 2 + step) % groups
+                rows = pl.ds(pl.multiple_of(group * quad * LANES, quad * LANES), quad * LANES)
+
+                def product(t):
+                    values = jnp.concatenate(
+                        [table[t, rows, :edge], table[t, rows, length - edge :]], axis=1
+                    )
+                    return lax.dot_general(
+                        values,
+                        spectra,
+                        (((1,), (1,)), ((), ())),
+                        preferred_element_type=jnp.float32,
+                    )
+
+                by_cosine = product(0)
+                by_sine = product(1)
+                real = (by_cosine[:, :LANES] - by_sine[:, LANES:]).astype(jnp.bfloat16)
+                imag = (by_sine[:, :LANES] + by_cosine[:, LANES:]).astype(jnp.bfloat16)
+                for q in range(quad):
+                    device = group * quad + q
+                    send[j, device, :LANES] = real[q * LANES : (q + 1) * LANES]
+                    send[j, device, LANES:] = imag[q * LANES : (q + 1) * LANES]
+
+                    @pl.when(device == me)
+                    def _():
+                        landing(j, me).start()
+
+                    @pl.when(device != me)
+                    def _():
+                        remote(j, device).start()
+
+    width = 512
+
+    def write(j):
+        return pltpu.make_async_copy(result.at[j % 2], out_hbm.at[j], out_sem.at[j % 2])
+
+    @pl.loop(0, slices)
+    def _(j):
+        @pl.loop(0, dead_first)
+        def _(source):
+            landing(j, source).wait()
+
+        @pl.loop(dead_last, count)
+        def _(source):
+            landing(j, source).wait()
+
+        @pl.when(j >= 2)
+        def _():
+            write(j - 2).wait()
+
+        @pl.loop(0, length // width)
+        def _(block):
+            cols = pl.ds(pl.multiple_of(block * width, width), width)
+            spectra = jnp.concatenate(
+                [recv[j, :, :edge], recv[j, :, length - edge :]], axis=1
+            )
+
+            def product(t):
+                values = jnp.concatenate(
+                    [table[t, :edge, cols], table[t, length - edge :, cols]], axis=0
+                )
+                return jnp.dot(spectra, values, preferred_element_type=jnp.float32)
+
+            by_cosine = product(0)
+            by_sine = product(1)
+            scale = 1.0 / length
+            result[j % 2, 0, :, cols] = (by_cosine[:LANES] - by_sine[LANES:]) * scale
+            result[j % 2, 1, :, cols] = (by_sine[:LANES] + by_cosine[LANES:]) * scale
+
+        write(j).start()
+
+    write(slices - 2).wait()
+    write(slices - 1).wait()
+
+    @pl.when(has_rows)
+    def _():
+        @pl.loop(0, slices)
+        def _(j):
+            @pl.loop(1, count)
+            def _(step):
+                remote(j, (me + step) % count).wait_send()
+
+
+def local_fast(residual_spectra, led_offsets, pupil_radius, led_axial, depths, slice_order, axial):
+    tile_rows, length = axial.shape
+    own_leds = residual_spectra.shape[0]
+    slices = depths.shape[0]
+    led_count = lax.axis_size("led")
+    led_index = lax.axis_index("led")
+    edge = useful_edge(length)
+    rows = tile_rows // led_count
+    swap = [(0, 1), (1, 0)]
+    other = lax.dynamic_slice_in_dim(residual_spectra, (1 - led_index) * rows, rows, axis=2)
+    other = jnp.concatenate([other[..., :edge], other[..., length - edge :]], axis=-1)
+    peer = lax.ppermute(other, "led", swap)
+    facts = jnp.concatenate(
+        [led_offsets.astype(jnp.float32).T, pupil_radius.astype(jnp.float32)[None], led_axial[None]]
+    )
+    facts = jnp.concatenate([facts, lax.ppermute(facts, "led", swap)], axis=1)
+    ordered = select_depths(slice_order, depths)
+    weights = mixing_weights(ordered, facts[3])
+    weights = weights.reshape(2 * slices, 2 * facts.shape[1])
+    eye = jnp.eye(GROUP, dtype=jnp.bfloat16)
+    weights = (weights[:, None, :, None] * eye[None, :, None, :]).reshape(
+        2 * slices * GROUP, 2 * facts.shape[1] * GROUP
+    )
+    whole = facts[:3].astype(jnp.int32)
+    first_row = lax.axis_index("tile") * tile_rows + led_index * rows
+    ints = jnp.concatenate(
+        [jnp.stack([led_index, first_row]), whole[0], whole[1], whole[2] * whole[2]]
+    )
+    steps = rows // GROUP
+    phased = pl.pallas_call(
+        functools.partial(mix_kernel, length, edge),
+        grid_spec=pltpu.PrefetchScalarGridSpec(
+            num_scalar_prefetch=2,
+            grid=(steps,),
+            in_specs=[
+                pl.BlockSpec(weights.shape, lambda g, s, d: (0, 0)),
+                pl.BlockSpec(
+                    (own_leds, 2, GROUP, length), lambda g, s, d: (0, 0, s[0] * steps + g, 0)
+                ),
+                pl.BlockSpec((own_leds, 2, GROUP, 2 * edge), lambda g, s, d: (0, 0, g, 0)),
+                pl.BlockSpec((GROUP, length), lambda g, s, d: (s[0] * steps + g, 0)),
+            ],
+            out_specs=pl.BlockSpec((slices, 2, GROUP, 2 * edge), lambda g, s, d: (0, 0, g, 0)),
+        ),
+        out_shape=jax.ShapeDtypeStruct((slices, 2, rows, 2 * edge), jnp.bfloat16),
+        compiler_params=pltpu.CompilerParams(vmem_limit_bytes=48 * 2**20),
+        name="mix",
+    )(ints, ordered, weights, residual_spectra, peer, axial)
+    phased = phased.reshape(slices, 2 * rows, 2 * edge)
+    count = length // LANES
+    bf16 = jnp.bfloat16
+    return pl.pallas_call(
+        functools.partial(transform_kernel, length, edge),
+        in_specs=[pl.BlockSpec(memory_space=pl.ANY)] * 2,
+        out_specs=pl.BlockSpec(memory_space=pl.ANY),
+        out_shape=jax.ShapeDtypeStruct((slices, 2, LANES, length), jnp.float32),
+        scratch_shapes=[
+            pltpu.VMEM((2, length, length), bf16),
+            pltpu.VMEM(phased.shape, bf16),
+            pltpu.VMEM((slices, count, 2 * LANES, LANES), bf16),
+            pltpu.VMEM((slices, 2 * LANES, length), bf16),
+            pltpu.VMEM((2, 2, LANES, length), jnp.float32),
+            pltpu.SemaphoreType.DMA,
+            pltpu.SemaphoreType.DMA,
+            pltpu.SemaphoreType.DMA((slices, count)),
+            pltpu.SemaphoreType.DMA((slices, count)),
+            pltpu.SemaphoreType.DMA((2,)),
+        ],
+        compiler_params=pltpu.CompilerParams(
+            collective_id=0, has_side_effects=True, vmem_limit_bytes=60 * 2**20
+        ),
+        name="transform",
+    )(jnp.asarray(full_table(length)), phased)
+
+
+def local_any(*arrays):
+    tile_rows, length = arrays[-1].shape
+    led_count = lax.axis_size("led")
+    if led_count == 2 and tile_rows == 2 * LANES and length % (8 * LANES) == 0:
+        return local_fast(*arrays)
+    return local(*arrays)
+
+
 def solution(mesh):
     placed = (
         P(("parts", "led"), None, "tile", None),
@@ -120,7 +427,7 @@
         P("tile", None),
     )
     return jax.shard_map(
-        local,
+        local_any,
         mesh=mesh,
         in_specs=placed,
         out_specs=P("parts", None, ("tile", "led"), None),

time: 652 us -> 258 us (0.40); the launches traced: 639 us -> 257 us
  Pallas kernels: 0 us -> 217 us
  blocking collectives: 206 us -> 0 us
  other arithmetic: 155 us -> 8.91 us
  local copies, waits for them, and re-layouts: 148 us -> 23.9 us
  matrix products: 117 us -> 0.18 us
  between operations: 14.6 us -> 0.12 us
    pallas_call x0 -> x2, Pallas kernels: none -> 217 us  [the longest x1 200 us: local_fast(): pl.pallas_call(functools.partial(transform_kernel, length, edge), in_spec...]
    all_to_all x2 -> x0, blocking collectives: 206 us -> none  [the longest x1 187 us: local(): lax.all_to_all(half_done, 'tile', split_axis=2, concat_axis=3, tiled=True)]
    another operation x10 -> x1, other arithmetic: 118 us -> 0.11 us
    dot_general x17 -> x0, matrix products: 116 us -> none  [the longest x16 81.7 us: transform(): jnp.einsum(form, spectra, dft, preferred_element_type=jnp.float32)]
    all_to_all x5 -> x0, local copies, waits for them, and re-layouts: 60.9 us -> none  [the longest x3 41 us: local(): lax.all_to_all(half_done, 'tile', split_axis=2, concat_axis=3, tiled=True)]
    dot_general x1 -> x0, local copies, waits for them, and re-layouts: 32.2 us -> none  [local(): jnp.einsum('jolc,lcak->joak', weights, masked, preferred_element_type=jnp...]
    concatenate x1, local copies, waits for them, and re-layouts: 25 us -> 0.08 us  [local_fast(): jnp.concatenate([jnp.stack([led_index, first_row]), whole[0], whole[1], w...]
    select_n x3 -> x0, other arithmetic: 14.4 us -> none  [the longest x1 14.4 us: masked_spectra(): return jnp.where(inside[:, None], residual, jnp.zeros_like(residual))]
  transfers between devices with their start and end apart: 1 -> 2, of which waited for: 0 -> 1; matrix products, arithmetic and copies ran while one was open for 13% -> 3% of each run, Pallas kernels for 0% -> 0%
where the time goes in v1:
time: 258 us; the launch traced here: 257 us
  Pallas kernels  217 us (84%)
  local copies, waits for them, and re-layouts  23.9 us (9%)
  other arithmetic  8.91 us (3%)
  waiting for transfers between devices  6.13 us (2%)
    pallas_call x1, Pallas kernels, local_fast(): pl.pallas_call(functools.partial(transform_kernel, length, edge), in_spec...  200 us
    pallas_call x1, Pallas kernels, local_fast(): pl.pallas_call(functools.partial(mix_kernel, length, edge), grid_spec=plt...  17.2 us
    unnamed x15, local copies, waits for them, and re-layouts  11.8 us
    slice x1, local copies, waits for them, and re-layouts, local_fast(): other[..., :edge]  7.12 us
    concatenate x1, other arithmetic, local_fast(): jnp.concatenate([other[..., :edge], other[..., length - edge:]], axis=-1)  7.06 us
    ppermute x1, waiting for transfers between devices, local_fast(): facts = jnp.concatenate([facts, lax.ppermute(facts, 'led', swap)], axis=1)  6.12 us
  transfers between devices with their start and end apart: 2, of which 1 were waited for; matrix products, arithmetic and copies ran while one was open for 3% of the time, Pallas kernels for 0%

profile of v1, /device:TPU:10, one launch (start us, length us, event | category | flops | bytes accessed | tf_op | source)
XLA Modules:
  0.0 257.1 jit_solution(143381352208383932)
XLA Ops:
  0.0 0.0 copy-start
  0.0 7.1 %constant_dynamic-slice_fusion = (bf16[8,2,128,896]{3,2,1,0:T(8,128)(2,1)}, bf16[8,2,128,896]{3,2,1,0:T(8,128)(2,1)}) fusion(bf16[8,2,256,2048]{3,2,1,0:T(8,128)(2,1)} %own.1, s32[]{:T(128)S(6)} %select_n.3, s32[]{:T(128)S(6)} %add.8), kind=kLoop, calls=%fused_computation.20 | loop fusion | bytes 14680072 | tf_op jit(solution)/shard_map/slice | solution.py:346
  7.1 0.0 copy-start.5
  7.1 0.0 copy-start.4
  7.1 0.0 copy-start.3
  7.1 0.0 copy-start.6
  7.1 0.0 copy-start.2
  7.1 7.1 %pad_maximum_fusion = bf16[8,2,128,1792]{3,2,1,0:T(8,128)(2,1)} fusion(bf16[8,2,128,896]{3,2,1,0:T(8,128)(2,1)} %get-tuple-element.6, bf16[8,2,128,896]{3,2,1,0:T(8,128)(2,1)} %get-tuple-element.5), kind=kLoop, calls=%fused_computation | loop fusion | flops 14680064 | bytes 14680064 | tf_op jit(solution)/shard_map/concatenate | solution.py:346
  14.2 0.0 collective-permute-start.1
  14.2 0.0 copy-done.5
  14.2 0.0 copy-done.4
  14.2 0.0 copy-done.3
  14.3 0.6 collective-permute-start
  14.8 0.0 copy-done
  14.8 0.0 copy-done.6
  14.8 0.2 convolution_bitcast_fusion.depths
  15.0 6.1 %collective-permute-done = f32[4,8]{1,0:T(4,128)S(1)} collective-permute-done((f32[4,8]{1,0:T(4,128)S(1)}, f32[4,8]{1,0:T(4,128)S(1)}, u32[]{:S(2)}, u32[]{:S(2)}) %collective-permute-start) | collective-permute-done | bytes 160 | tf_op jit(solution)/shard_map/ppermute | solution.py:351
  21.1 0.1 pad_maximum_fusion.3
  21.2 0.1 fusion.2
  21.4 0.2 copy.11
  21.6 0.1 convert_element_type.28
  21.7 1.6 broadcast_multiply_fusion
  23.3 4.5 %mul.73.weights = bf16[256,512]{1,0:T(8,128)(2,1)S(1)} reshape(bf16[16,16,32,16]{3,2,1,0:T(8,128)(2,1)} %broadcast_multiply_fusion) | data formatting | bytes 524288 | tf_op jit(solution)/shard_map/mul | solution.py:356
  27.8 0.1 concatenate.14.ints
  27.9 0.0 collective-permute-done.1.peer
  27.9 0.0 copy-done.2
  27.9 17.2 %mix.1 = bf16[8,2,128,1792]{3,2,1,0:T(8,128)(2,1)} custom-call(s32[50]{0:T(128)S(1)} %concatenate.14.ints, f32[8]{0:T(128)S(1)} %convolution_bitcast_fusion.depths, bf16[256,512]{1,0:T(8,128)(2,1)S(1)} %mul.73.weights, bf16[8,2,256,2048]{3,2,1,0:T(8,128)(2,1)} %own.1, bf16[8,2,128,1792]{3,2,1,0:T(8,128)(2,1)} %collective-permute-done.1.peer, ...), custom_call_target="tpu_custom_call" | custom-call | tf_op jit(solution)/shard_map/mix/pallas_call | solution.py:365
  45.1 200.2 %transform.1 = f32[8,2,128,2048]{3,2,1,0:T(8,128)} custom-call(bf16[2,2048,2048]{2,1,0:T(8,128)(2,1)} %constant.18.clone.table_hbm, bf16[8,256,1792]{2,1,0:T(8,128)(2,1)} %bitcast.29), custom_call_target="tpu_custom_call" | custom-call | tf_op jit(solution)/shard_map/transform/pallas_call | solution.py:387
  245.3 0.0 copy-start.1
  245.3 11.8 %copy.13 = f32[8,2,128,2048]{3,2,1,0:T(8,128)} copy(f32[8,2,128,2048]{3,2,1,0:T(8,128)} %transform.1) | data formatting | bytes 33554432
  257.1 0.0 copy-done.1
  (9 shorter events, 0.1 us)
Async XLA Ops:
  0.0 14.8 %copy-start = (f32[8]{0:T(128)S(1)}, f32[8]{0:T(128)}, u32[]{:S(2)}) copy-start(f32[8]{0:T(128)} %param.12) | copy-start | bytes 100
  7.1 7.1 %copy-start.5 = (s32[8]{0:T(128)S(1)}, s32[8]{0:T(128)}, u32[]{:S(2)}) copy-start(s32[8]{0:T(128)} %param.10) | copy-start | bytes 100
  7.1 7.1 %copy-start.4 = (s32[8,2]{0,1:T(2,128)S(1)}, s32[8,2]{0,1:T(2,128)}, u32[]{:S(2)}) copy-start(s32[8,2]{0,1:T(2,128)} %param.9) | copy-start | bytes 196
  7.1 7.1 %copy-start.3 = (f32[8]{0:T(128)S(1)}, f32[8]{0:T(128)}, u32[]{:S(2)}) copy-start(f32[8]{0:T(128)} %param.11) | copy-start | bytes 100
  7.1 7.7 %copy-start.6 = (s32[8]{0:T(128)S(1)}, s32[8]{0:T(128)}, u32[]{:S(2)}) copy-start(s32[8]{0:T(128)} %param.13) | copy-start | bytes 100
  7.1 20.8 %copy-start.2 = (f32[256,2048]{1,0:T(8,128)S(1)}, f32[256,2048]{1,0:T(8,128)}, u32[]{:S(2)}) copy-start(f32[256,2048]{1,0:T(8,128)} %axial.1) | copy-start | bytes 6291460
  14.2 13.7 %collective-permute-start.1 = (bf16[8,2,128,1792]{3,2,1,0:T(8,128)(2,1)}, bf16[8,2,128,1792]{3,2,1,0:T(8,128)(2,1)}, u32[]{:S(2)}, u32[]{:S(2)}) collective-permute-start(bf16[8,2,128,1792]{3,2,1,0:T(8,128)(2,1)} %pad_maximum_fusion), channel_id=1, source_target_pairs={{0,1},{1,0},{2,3},{3,2},{4,5},{5,4},{6,7},{7,6},{8,9},{9,8},{10,11... | collective-permute-start | bytes 22020104 | tf_op jit(solution)/shard_map/ppermute | solution.py:347
  14.3 6.9 %collective-permute-start = (f32[4,8]{1,0:T(4,128)S(1)}, f32[4,8]{1,0:T(4,128)S(1)}, u32[]{:S(2)}, u32[]{:S(2)}) collective-permute-start(f32[4,8]{1,0:T(4,128)S(1)} %pad_maximum_fusion.2), channel_id=1, source_target_pairs={{0,1},{1,0},{2,3},{3,2},{4,5},{5,4},{6,7},{7,6},{8,9},{9,8},{10,11... | collective-permute-start | bytes 392 | tf_op jit(solution)/shard_map/ppermute | solution.py:351
  245.3 11.8 %copy-start.1 = (f32[8]{0:T(128)S(1)}, f32[8]{0:T(128)}, u32[]{:S(2)}) copy-start(f32[8]{0:T(128)} %param.12) | copy-start | bytes 100

commit v2 on v1

--- a/solution.py
+++ b/solution.py
@@ -142,11 +142,28 @@
     return sine, cosine
 
 
-def mix_kernel(length, edge, ints, depths, weights, own, peer, axial, out):
+def spread_weights(weights, spread):
+    height, depth = weights.shape
+    shape = (depth, depth * GROUP)
+    picks = lax.broadcasted_iota(jnp.int32, shape, 1) // GROUP == lax.broadcasted_iota(
+        jnp.int32, shape, 0
+    )
+    picks = jnp.where(picks, 1.0, 0.0).astype(jnp.bfloat16)
+    wide = jnp.dot(weights[...], picks, preferred_element_type=jnp.float32)
+    shape = (GROUP, depth * GROUP)
+    diagonal = lax.broadcasted_iota(jnp.int32, shape, 1) % GROUP == lax.broadcasted_iota(
+        jnp.int32, shape, 0
+    )
+    for row in range(height):
+        block = jnp.where(diagonal, jnp.broadcast_to(wide[row : row + 1], shape), 0.0)
+        spread[row * GROUP : (row + 1) * GROUP] = block.astype(jnp.bfloat16)
+
+
+def mix_group(length, edge, row_start, ints, depths, spread, own, peer, axial, store):
     own_leds, peer_leds = own.shape[0], peer.shape[0]
     leds = own_leds + peer_leds
-    slices = out.shape[0]
-    row = ints[1] + pl.program_id(0) * GROUP + lax.broadcasted_iota(jnp.int32, (GROUP, 1), 0)
+    slices = depths.shape[0]
+    row = row_start + lax.broadcasted_iota(jnp.int32, (GROUP, 1), 0)
     freq_row = jnp.where(row < length // 2, row, row - length)
     lane = lax.broadcasted_iota(jnp.int32, (1, edge), 1)
     for half in range(2):
@@ -154,9 +171,9 @@
         freq_col = lane if half == 0 else lane - edge
         planes = []
         for led in range(leds):
-            shift_row = freq_row - ints[2 + led]
-            shift_col = freq_col - ints[2 + leds + led]
-            room = ints[2 + 2 * leds + led] - shift_row * shift_row
+            shift_row = freq_row - ints[led]
+            shift_col = freq_col - ints[leds + led]
+            room = ints[2 * leds + led] - shift_row * shift_row
             inside = jnp.where(shift_col * shift_col <= room, 1.0, 0.0).astype(jnp.bfloat16)
             for part in range(2):
                 if led < own_leds:
@@ -165,30 +182,41 @@
                     values = peer[led - own_leds, part, :, half * edge : (half + 1) * edge]
                 planes.append(values * inside)
         stacked = jnp.concatenate(planes, axis=0)
-        summed = jnp.dot(weights[...], stacked, preferred_element_type=jnp.float32)
+        summed = jnp.dot(spread[...], stacked, preferred_element_type=jnp.float32)
         wave = axial[:, start : start + edge]
         for j in range(slices):
             real = summed[(2 * j) * GROUP : (2 * j + 1) * GROUP]
             imag = summed[(2 * j + 1) * GROUP : (2 * j + 2) * GROUP]
             sine, cosine = sine_cosine(depths[j] * wave)
             where = slice(half * edge, (half + 1) * edge)
-            out[j, 0, :, where] = (real * cosine - imag * sine).astype(jnp.bfloat16)
-            out[j, 1, :, where] = (real * sine + imag * cosine).astype(jnp.bfloat16)
+            store(j, 0, where, (real * cosine - imag * sine).astype(jnp.bfloat16))
+            store(j, 1, where, (real * sine + imag * cosine).astype(jnp.bfloat16))
 
 
 def transform_kernel(
     length,
     edge,
+    ints,
+    depths,
+    weights,
     table_hbm,
-    phased_hbm,
+    spectra_hbm,
+    axial_hbm,
     out_hbm,
     table,
     phased,
+    spread,
+    own,
+    peer,
+    axial,
     send,
     recv,
     result,
-    load_sem,
-    phased_sem,
+    table_sem,
+    own_sem,
+    axial_sem,
+    peer_send_sem,
+    peer_recv_sem,
     send_sem,
     recv_sem,
     out_sem,
@@ -203,10 +231,47 @@
     def place(device):
         return (part, device // led_count, device % led_count)
 
-    table_load = pltpu.make_async_copy(table_hbm, table, load_sem)
-    table_load.start()
-    phased_load = pltpu.make_async_copy(phased_hbm, phased, phased_sem)
-    phased_load.start()
+    led_index = lax.axis_index("led")
+    rows = axial.shape[0]
+    first_row = me * rows
+    steps = rows // GROUP
+    quad = 4
+    groups = count // quad
+    partner = (part, me // led_count, 1 - led_index)
+
+    def load_own(step):
+        here = pl.ds(pl.multiple_of(led_index * rows + step * GROUP, GROUP), GROUP)
+        return pltpu.make_async_copy(
+            spectra_hbm.at[:, :, here], own.at[step % 2], own_sem.at[step % 2]
+        )
+
+    def load_axial():
+        here = pl.ds(pl.multiple_of(led_index * rows, GROUP), rows)
+        return pltpu.make_async_copy(axial_hbm.at[here], axial, axial_sem)
+
+    def rows_of(group):
+        return pl.ds(pl.multiple_of(group * quad * LANES, quad * LANES), quad * LANES)
+
+    def load_table(step):
+        there = rows_of((me // quad + groups // 2 + step) % groups)
+        return pltpu.make_async_copy(
+            table_hbm.at[:, there], table.at[:, there], table_sem.at[step]
+        )
+
+    def swap(step, half):
+        there = pl.ds(pl.multiple_of((1 - led_index) * rows + step * GROUP, GROUP), GROUP)
+        start = 0 if half == 0 else length - edge
+        return pltpu.make_async_remote_copy(
+            src_ref=spectra_hbm.at[:, :, there, start : start + edge],
+            dst_ref=peer.at[step, :, :, :, half * edge : (half + 1) * edge],
+            send_sem=peer_send_sem.at[step, half],
+            recv_sem=peer_recv_sem.at[step, half],
+            device_id=partner,
+            device_id_type=MESH,
+        )
+
+    load_own(0).start()
+    load_axial().start()
 
     barrier = pltpu.get_barrier_semaphore()
 
@@ -217,8 +282,50 @@
         )
 
     pl.semaphore_wait(barrier, count - 1)
-    phased_load.wait()
-    table_load.wait()
+
+    @pl.loop(0, steps)
+    def _(step):
+        swap(step, 0).start()
+        swap(step, 1).start()
+
+    @pl.loop(0, groups)
+    def _(step):
+        load_table(step).start()
+
+    spread_weights(weights, spread)
+    load_axial().wait()
+
+    @pl.loop(0, steps)
+    def _(step):
+        @pl.when(step + 1 < steps)
+        def _():
+            load_own(step + 1).start()
+
+        load_own(step).wait()
+        swap(step, 0).wait_recv()
+        swap(step, 1).wait_recv()
+        here = pl.ds(pl.multiple_of(step * GROUP, GROUP), GROUP)
+
+        def store(j, half, where, values):
+            there = pl.ds(pl.multiple_of(half * rows + step * GROUP, GROUP), GROUP)
+            phased[j, there, where] = values
+
+        mix_group(
+            length,
+            edge,
+            first_row + step * GROUP,
+            ints,
+            depths,
+            spread,
+            own.at[step % 2],
+            peer.at[step],
+            axial.at[here],
+            store,
+        )
+
+    @pl.loop(0, groups)
+    def _(step):
+        load_table(step).wait()
 
     def lanes_of(device):
         return pl.ds(pl.multiple_of(device * LANES, LANES), LANES)
@@ -239,8 +346,6 @@
         )
 
     has_rows = jnp.logical_or(me < dead_first, me >= dead_last)
-    quad = 4
-    groups = count // quad
 
     @pl.when(has_rows)
     def _():
@@ -251,11 +356,11 @@
             @pl.loop(0, groups)
             def _(step):
                 group = (me // quad + groups // 2 + step) % groups
-                rows = pl.ds(pl.multiple_of(group * quad * LANES, quad * LANES), quad * LANES)
+                here = rows_of(group)
 
                 def product(t):
                     values = jnp.concatenate(
-                        [table[t, rows, :edge], table[t, rows, length - edge :]], axis=1
+                        [table[t, here, :edge], table[t, here, length - edge :]], axis=1
                     )
                     return lax.dot_general(
                         values,
@@ -324,6 +429,11 @@
     write(slices - 2).wait()
     write(slices - 1).wait()
 
+    @pl.loop(0, steps)
+    def _(step):
+        swap(step, 0).wait_send()
+        swap(step, 1).wait_send()
+
     @pl.when(has_rows)
     def _():
         @pl.loop(0, slices)
@@ -337,75 +447,51 @@
     tile_rows, length = axial.shape
     own_leds = residual_spectra.shape[0]
     slices = depths.shape[0]
-    led_count = lax.axis_size("led")
-    led_index = lax.axis_index("led")
     edge = useful_edge(length)
-    rows = tile_rows // led_count
-    swap = [(0, 1), (1, 0)]
-    other = lax.dynamic_slice_in_dim(residual_spectra, (1 - led_index) * rows, rows, axis=2)
-    other = jnp.concatenate([other[..., :edge], other[..., length - edge :]], axis=-1)
-    peer = lax.ppermute(other, "led", swap)
+    rows = tile_rows // lax.axis_size("led")
     facts = jnp.concatenate(
         [led_offsets.astype(jnp.float32).T, pupil_radius.astype(jnp.float32)[None], led_axial[None]]
     )
-    facts = jnp.concatenate([facts, lax.ppermute(facts, "led", swap)], axis=1)
+    facts = jnp.concatenate([facts, lax.ppermute(facts, "led", [(0, 1), (1, 0)])], axis=1)
+    leds = facts.shape[1]
     ordered = select_depths(slice_order, depths)
-    weights = mixing_weights(ordered, facts[3])
-    weights = weights.reshape(2 * slices, 2 * facts.shape[1])
-    eye = jnp.eye(GROUP, dtype=jnp.bfloat16)
-    weights = (weights[:, None, :, None] * eye[None, :, None, :]).reshape(
-        2 * slices * GROUP, 2 * facts.shape[1] * GROUP
-    )
+    weights = mixing_weights(ordered, facts[3]).reshape(2 * slices, 2 * leds)
     whole = facts[:3].astype(jnp.int32)
-    first_row = lax.axis_index("tile") * tile_rows + led_index * rows
-    ints = jnp.concatenate(
-        [jnp.stack([led_index, first_row]), whole[0], whole[1], whole[2] * whole[2]]
-    )
+    ints = jnp.concatenate([whole[0], whole[1], whole[2] * whole[2]])
+    count = length // LANES
     steps = rows // GROUP
-    phased = pl.pallas_call(
-        functools.partial(mix_kernel, length, edge),
-        grid_spec=pltpu.PrefetchScalarGridSpec(
-            num_scalar_prefetch=2,
-            grid=(steps,),
-            in_specs=[
-                pl.BlockSpec(weights.shape, lambda g, s, d: (0, 0)),
-                pl.BlockSpec(
-                    (own_leds, 2, GROUP, length), lambda g, s, d: (0, 0, s[0] * steps + g, 0)
-                ),
-                pl.BlockSpec((own_leds, 2, GROUP, 2 * edge), lambda g, s, d: (0, 0, g, 0)),
-                pl.BlockSpec((GROUP, length), lambda g, s, d: (s[0] * steps + g, 0)),
-            ],
-            out_specs=pl.BlockSpec((slices, 2, GROUP, 2 * edge), lambda g, s, d: (0, 0, g, 0)),
-        ),
-        out_shape=jax.ShapeDtypeStruct((slices, 2, rows, 2 * edge), jnp.bfloat16),
-        compiler_params=pltpu.CompilerParams(vmem_limit_bytes=48 * 2**20),
-        name="mix",
-    )(ints, ordered, weights, residual_spectra, peer, axial)
-    phased = phased.reshape(slices, 2 * rows, 2 * edge)
-    count = length // LANES
     bf16 = jnp.bfloat16
+    smem = pl.BlockSpec(memory_space=pltpu.SMEM)
     return pl.pallas_call(
         functools.partial(transform_kernel, length, edge),
-        in_specs=[pl.BlockSpec(memory_space=pl.ANY)] * 2,
+        in_specs=[smem, smem, pl.BlockSpec(memory_space=pltpu.VMEM)]
+        + [pl.BlockSpec(memory_space=pl.ANY)] * 3,
         out_specs=pl.BlockSpec(memory_space=pl.ANY),
         out_shape=jax.ShapeDtypeStruct((slices, 2, LANES, length), jnp.float32),
         scratch_shapes=[
             pltpu.VMEM((2, length, length), bf16),
-            pltpu.VMEM(phased.shape, bf16),
+            pltpu.VMEM((slices, 2 * rows, 2 * edge), bf16),
+            pltpu.VMEM((2 * slices * GROUP, 2 * leds * GROUP), bf16),
+            pltpu.VMEM((2, own_leds, 2, GROUP, length), bf16),
+            pltpu.VMEM((steps, own_leds, 2, GROUP, 2 * edge), bf16),
+            pltpu.VMEM((rows, length), jnp.float32),
             pltpu.VMEM((slices, count, 2 * LANES, LANES), bf16),
             pltpu.VMEM((slices, 2 * LANES, length), bf16),
             pltpu.VMEM((2, 2, LANES, length), jnp.float32),
+            pltpu.SemaphoreType.DMA((count // 4,)),
+            pltpu.SemaphoreType.DMA((2,)),
             pltpu.SemaphoreType.DMA,
-            pltpu.SemaphoreType.DMA,
+            pltpu.SemaphoreType.DMA((steps, 2)),
+            pltpu.SemaphoreType.DMA((steps, 2)),
             pltpu.SemaphoreType.DMA((slices, count)),
             pltpu.SemaphoreType.DMA((slices, count)),
             pltpu.SemaphoreType.DMA((2,)),
         ],
         compiler_params=pltpu.CompilerParams(
-            collective_id=0, has_side_effects=True, vmem_limit_bytes=60 * 2**20
+            collective_id=0, has_side_effects=True, vmem_limit_bytes=61 * 2**20
         ),
         name="transform",
-    )(jnp.asarray(full_table(length)), phased)
+    )(ints, ordered, weights, jnp.asarray(full_table(length)), residual_spectra, axial)
 
 
 def local_any(*arrays):

time: 258 us -> 233 us (0.903)
  local copies, waits for them, and re-layouts: 23.9 us -> 12.7 us
  waiting for transfers between devices: 6.13 us -> 0.3 us
  other arithmetic: 8.91 us -> 3.46 us
  Pallas kernels: 217 us -> 213 us
    pallas_call x1 -> x0, Pallas kernels: 17.2 us -> none  [local_fast(): pl.pallas_call(functools.partial(mix_kernel, length, edge), grid_spec=plt...]
    pallas_call x1, Pallas kernels: 200 us -> 213 us  [local_fast(): pl.pallas_call(functools.partial(transform_kernel, length, edge), in_spec...]
    slice x1 -> x0, local copies, waits for them, and re-layouts: 7.12 us -> none  [local_fast(): other[..., :edge]]
    concatenate x2, other arithmetic: 7.14 us -> 1.31 us  [the longest x1 0.73 us: local_fast(): jnp.concatenate([facts, lax.ppermute(facts, 'led', [(0, 1), (1, 0)])], ax...]
    ppermute x2 -> x1, waiting for transfers between devices: 6.13 us -> 0.3 us  [local_fast(): lax.ppermute(facts, 'led', [(0, 1), (1, 0)])]
    mul x1 -> x0, local copies, waits for them, and re-layouts: 4.51 us -> none  [local_fast(): weights[:, None, :, None] * eye[None, :, None, :]]
    unnamed x15 -> x7, local copies, waits for them, and re-layouts: 11.8 us -> 11.8 us
  transfers between devices with their start and end apart: 2 -> 1, of which waited for: 1 -> 1; matrix products, arithmetic and copies ran while one was open for 3% -> 0% of each run, Pallas kernels for 0% -> 0%
where the time goes in v2:
time: 233 us; the launch traced here: 231 us
  Pallas kernels  213 us (91%)
  local copies, waits for them, and re-layouts  12.7 us (5%)
  other arithmetic  3.46 us (1%)
    pallas_call x1, Pallas kernels, local_fast(): pl.pallas_call(functools.partial(transform_kernel, length, edge), in_spec...  213 us
    unnamed x7, local copies, waits for them, and re-layouts  11.8 us
  transfers between devices with their start and end apart: 1, of which 1 were waited for; matrix products, arithmetic and copies ran while one was open for 0% of the time, Pallas kernels for 0%

profile of v2, /device:TPU:10, one launch (start us, length us, event | category | flops | bytes accessed | tf_op | source)
XLA Modules:
  0.0 230.8 jit_solution(13308936990261147444)
XLA Ops:
  0.0 0.0 copy-start
  0.0 0.7 convert_bitcast_fusion.1
  0.7 0.7 convert_bitcast_fusion
  1.4 0.7 pad_maximum_fusion.1
  2.0 0.0 collective-permute-start
  2.0 0.0 copy-done
  2.0 0.8 convolution_bitcast_fusion.depths
  2.9 0.0 copy-start.2
  2.9 0.3 collective-permute-done
  3.2 0.7 pad_maximum_fusion.2
  3.9 0.1 fusion.1
  4.1 0.2 copy.11
  4.3 0.7 convert_element_type.18.weights
  5.0 0.6 pad_add_fusion.ints
  5.6 0.0 copy-done.2
  5.6 0.0 copy-start.1
  5.6 213.4 %transform.1 = f32[8,2,128,2048]{3,2,1,0:T(8,128)} custom-call(s32[48]{0:T(128)} %pad_add_fusion.ints, f32[8]{0:T(128)} %copy-done.2, bf16[16,32]{1,0:T(8,128)(2,1)} %convert_element_type.18.weights, bf16[2,2048,2048]{2,1,0:T(8,128)(2,1)} %constant.2.clone.table_hbm, bf16[8,2,256,2048]{3,2,1,0:T(8,128)(2,1)} %spectra_hbm.1, f32[256,2048]{1,0:T(8,128)} %axial_hbm.1), custom_call_target="tpu_custom_call" | custom-call | tf_op jit(solution)/shard_map/transform/pallas_call | solution.py:465
  219.0 11.8 %copy.13 = f32[8,2,128,2048]{3,2,1,0:T(8,128)} copy(f32[8,2,128,2048]{3,2,1,0:T(8,128)} %transform.1) | data formatting | bytes 33554432
  230.8 0.0 copy-done.1
  (5 shorter events, 0.0 us)
Async XLA Ops:
  0.0 2.0 copy-start
  2.0 1.2 collective-permute-start
  2.9 2.7 %copy-start.2 = (f32[8]{0:T(128)}, f32[8]{0:T(128)S(1)}, u32[]{:S(2)}) copy-start(f32[8]{0:T(128)S(1)} %convolution_bitcast_fusion.depths) | copy-start | bytes 100
  5.6 225.3 %copy-start.1 = (f32[8]{0:T(128)S(1)}, f32[8]{0:T(128)}, u32[]{:S(2)}) copy-start(f32[8]{0:T(128)} %param.12) | copy-start | bytes 100

commit v3 on v2

--- a/solution.py
+++ b/solution.py
@@ -219,11 +219,15 @@
     peer_recv_sem,
     send_sem,
     recv_sem,
+    hand_send_sem,
+    hand_recv_sem,
     out_sem,
 ):
     slices = phased.shape[0]
     count = length // LANES
     dead_first, dead_last = edge // LANES, count - edge // LANES
+    half_count = count // 2
+    handed_slices = slices // 2
     led_count = lax.axis_size("led")
     part = lax.axis_index("parts")
     me = lax.axis_index("tile") * led_count + lax.axis_index("led")
@@ -249,11 +253,15 @@
         here = pl.ds(pl.multiple_of(led_index * rows, GROUP), rows)
         return pltpu.make_async_copy(axial_hbm.at[here], axial, axial_sem)
 
+    def group_of(step):
+        mine = me // quad
+        return (mine // 2 + 1 + step // 2) % 2 * 2 + (mine + step + step // 2) % 2
+
     def rows_of(group):
         return pl.ds(pl.multiple_of(group * quad * LANES, quad * LANES), quad * LANES)
 
     def load_table(step):
-        there = rows_of((me // quad + groups // 2 + step) % groups)
+        there = rows_of(group_of(step))
         return pltpu.make_async_copy(
             table_hbm.at[:, there], table.at[:, there], table_sem.at[step]
         )
@@ -345,6 +353,40 @@
             send.at[j, device], recv.at[j, :, lanes_of(device)], recv_sem.at[j, device]
         )
 
+    side = me // half_count
+    far = pl.multiple_of((1 - side) * half_count, half_count)
+    carrier = dead_first + side
+    sender = carrier - 2 + 4 * side
+    is_sender = me == sender
+    is_carrier = me == carrier
+
+    def hand_over(j):
+        return pltpu.make_async_remote_copy(
+            src_ref=send.at[j, pl.ds(far, half_count)],
+            dst_ref=send.at[j, pl.ds(far, half_count)],
+            send_sem=hand_send_sem.at[j],
+            recv_sem=hand_recv_sem.at[j],
+            device_id=place(carrier),
+            device_id_type=MESH,
+        )
+
+    def handed(j):
+        return pltpu.make_async_copy(
+            send.at[j, pl.ds(far, half_count)],
+            send.at[j, pl.ds(far, half_count)],
+            hand_recv_sem.at[j],
+        )
+
+    def forward(j, device):
+        return pltpu.make_async_remote_copy(
+            src_ref=send.at[j, device],
+            dst_ref=recv.at[j, :, lanes_of(sender)],
+            send_sem=send_sem.at[j, device],
+            recv_sem=recv_sem.at[j, sender],
+            device_id=place(device),
+            device_id_type=MESH,
+        )
+
     has_rows = jnp.logical_or(me < dead_first, me >= dead_last)
 
     @pl.when(has_rows)
@@ -352,10 +394,11 @@
         @pl.loop(0, slices)
         def _(j):
             spectra = phased[j]
+            hands = jnp.logical_and(is_sender, j < handed_slices)
 
             @pl.loop(0, groups)
             def _(step):
-                group = (me // quad + groups // 2 + step) % groups
+                group = group_of(step)
                 here = rows_of(group)
 
                 def product(t):
@@ -382,9 +425,27 @@
                     def _():
                         landing(j, me).start()
 
-                    @pl.when(device != me)
+                    @pl.when(
+                        jnp.logical_and(
+                            device != me, jnp.logical_not(jnp.logical_and(hands, step < 2))
+                        )
+                    )
                     def _():
                         remote(j, device).start()
+
+                @pl.when(jnp.logical_and(hands, step == 1))
+                def _():
+                    hand_over(j).start()
+
+    @pl.when(is_carrier)
+    def _():
+        @pl.loop(0, handed_slices)
+        def _(j):
+            handed(j).wait()
+
+            @pl.loop(0, half_count)
+            def _(device):
+                forward(j, far + device).start()
 
     width = 512
 
@@ -438,9 +499,27 @@
     def _():
         @pl.loop(0, slices)
         def _(j):
+            hands = jnp.logical_and(is_sender, j < handed_slices)
+
             @pl.loop(1, count)
             def _(step):
-                remote(j, (me + step) % count).wait_send()
+                device = (me + step) % count
+
+                @pl.when(jnp.logical_not(jnp.logical_and(hands, device // half_count != side)))
+                def _():
+                    remote(j, device).wait_send()
+
+            @pl.when(hands)
+            def _():
+                hand_over(j).wait_send()
+
+    @pl.when(is_carrier)
+    def _():
+        @pl.loop(0, handed_slices)
+        def _(j):
+            @pl.loop(0, half_count)
+            def _(device):
+                forward(j, far + device).wait_send()
 
 
 def local_fast(residual_spectra, led_offsets, pupil_radius, led_axial, depths, slice_order, axial):
@@ -485,6 +564,8 @@
             pltpu.SemaphoreType.DMA((steps, 2)),
             pltpu.SemaphoreType.DMA((slices, count)),
             pltpu.SemaphoreType.DMA((slices, count)),
+            pltpu.SemaphoreType.DMA((slices,)),
+            pltpu.SemaphoreType.DMA((slices,)),
             pltpu.SemaphoreType.DMA((2,)),
         ],
         compiler_params=pltpu.CompilerParams(
@@ -497,7 +578,7 @@
 def local_any(*arrays):
     tile_rows, length = arrays[-1].shape
     led_count = lax.axis_size("led")
-    if led_count == 2 and tile_rows == 2 * LANES and length % (8 * LANES) == 0:
+    if led_count == 2 and tile_rows == 2 * LANES and length == 16 * LANES:
         return local_fast(*arrays)
     return local(*arrays)
 

time: 233 us -> 213 us (0.914)
  Pallas kernels: 213 us -> 196 us
    pallas_call x1, Pallas kernels: 213 us -> 196 us  [local_fast(): pl.pallas_call(functools.partial(transform_kernel, length, edge), in_spec...]
where the time goes in v3:
time: 213 us
  Pallas kernels  196 us (92%)
  local copies, waits for them, and re-layouts  12.7 us (6%)
  other arithmetic  3.46 us (2%)
    pallas_call x1, Pallas kernels, local_fast(): pl.pallas_call(functools.partial(transform_kernel, length, edge), in_spec...  196 us
    unnamed x7, local copies, waits for them, and re-layouts  11.8 us
  transfers between devices with their start and end apart: 1, of which 1 were waited for; matrix products, arithmetic and copies ran while one was open for 0% of the time, Pallas kernels for 0%

profile of v3, /device:TPU:10, one launch (start us, length us, event | category | flops | bytes accessed | tf_op | source)
XLA Modules:
  0.0 212.9 jit_solution(14228818364659632221)
XLA Ops:
  0.0 0.0 copy-start
  0.0 0.7 convert_bitcast_fusion.1
  0.7 0.7 convert_bitcast_fusion
  1.4 0.7 pad_maximum_fusion.1
  2.0 0.0 collective-permute-start
  2.0 0.0 copy-done
  2.0 0.8 convolution_bitcast_fusion.depths
  2.9 0.0 copy-start.2
  2.9 0.3 collective-permute-done
  3.2 0.7 pad_maximum_fusion.2
  3.9 0.1 fusion.1
  4.1 0.2 copy.11
  4.3 0.7 convert_element_type.18.weights
  5.0 0.6 pad_add_fusion.ints
  5.6 0.0 copy-done.2
  5.6 0.0 copy-start.1
  5.6 195.6 %transform.1 = f32[8,2,128,2048]{3,2,1,0:T(8,128)} custom-call(s32[48]{0:T(128)} %pad_add_fusion.ints, f32[8]{0:T(128)} %copy-done.2, bf16[16,32]{1,0:T(8,128)(2,1)} %convert_element_type.18.weights, bf16[2,2048,2048]{2,1,0:T(8,128)(2,1)} %constant.2.clone.table_hbm, bf16[8,2,256,2048]{3,2,1,0:T(8,128)(2,1)} %spectra_hbm.1, f32[256,2048]{1,0:T(8,128)} %axial_hbm.1), custom_call_target="tpu_custom_call" | custom-call | tf_op jit(solution)/shard_map/transform/pallas_call | solution.py:544
  201.1 11.8 %copy.13 = f32[8,2,128,2048]{3,2,1,0:T(8,128)} copy(f32[8,2,128,2048]{3,2,1,0:T(8,128)} %transform.1) | data formatting | bytes 33554432
  212.9 0.0 copy-done.1
  (5 shorter events, 0.0 us)
Async XLA Ops:
  0.0 2.0 copy-start
  2.0 1.2 collective-permute-start
  2.9 2.7 %copy-start.2 = (f32[8]{0:T(128)}, f32[8]{0:T(128)S(1)}, u32[]{:S(2)}) copy-start(f32[8]{0:T(128)S(1)} %convolution_bitcast_fusion.depths) | copy-start | bytes 100
  5.6 207.4 %copy-start.1 = (f32[8]{0:T(128)S(1)}, f32[8]{0:T(128)}, u32[]{:S(2)}) copy-start(f32[8]{0:T(128)} %param.12) | copy-start | bytes 100
